TPU v7x, 256 devices: a whole 4x4x8 slice. The times are simulated.
256 devices in a mesh: vox: 32 (over z, y), col: 8 (over x, core).
Axes of the slice: x: 4, y: 4, z: 8, core: 2. Of those that a mesh axis runs over, the one named last changes fastest.
Arguments:
- start_modes: float32 [128, 131072], P('col', 'vox'), may hold values from -48 to 48
- start_dirs: float32 [128, 131072], P('col', 'vox'), may hold values from -6 to 6
- coupling: float32 [13, 131072], P(None, ('vox', 'col')), may hold values from 0.05 to 1
- relax_class: int32 [131072], P(('vox', 'col')), may hold values from 0 to 3
- relaxivity: float32 [4], replicated, may hold values from 0.5 to 4
Outputs:
- modes: float32 [128, 131072], P('col', 'vox')
- ritz: float32 [128, 128], replicated
All inputs are finite; a program needn't handle non-finite values.
Results may differ from a plain program's by a relative error of at most 0.0003.
Values sent between devices are 32-bit elements; how exact they have to be, the bound alone decides.
A program may use at most 64 MiB of HBM per device.

v0:
```python
import math
import jax
import jax.numpy as jnp
from jax import lax
from jax.sharding import PartitionSpec as P

NX = 256
NZ = 2
HALF = 13
ITERS = 2
QSTEPS = 3
offsets = [
    (a, b, c) for a in (-1, 0, 1) for b in (-1, 0, 1) for c in (-1, 0, 1) if (a, b, c) > (0, 0, 0)
]


def from_behind(block, axis, distance):
    devices = range(lax.axis_size(axis))
    route = [(i - distance, i) for i in devices if i - distance in devices]
    return lax.ppermute(block, axis, route)


def extended_2(block, sides, width):
    for axis, dim in sides:
        count = lax.axis_size(axis)
        forward = [(i, i + 1) for i in range(count - 1)]
        backward = [(target, source) for source, target in forward]
        low = lax.ppermute(
            lax.slice_in_dim(block, block.shape[dim] - width, None, axis=dim), axis, forward
        )
        high = lax.ppermute(lax.slice_in_dim(block, 0, width, axis=dim), axis, backward)
        block = jnp.concatenate([low, block, high], axis=dim)
    return block


def matmul(left, right):
    return jnp.dot(left, right, precision=lax.Precision.HIGHEST, preferred_element_type=jnp.float32)


def lower_solve(lower, rhs):
    return lax.linalg.triangular_solve(lower, rhs, left_side=True, lower=True)


def upper_solve(lower, rhs):
    return lax.linalg.triangular_solve(lower, rhs, left_side=True, lower=True, transpose_a=True)


def symmetric(matrix):
    return 0.5 * (matrix + matrix.T)


def project_pencil(gram_a, gram_b, count):
    sym_a = symmetric(gram_a)
    scales = lax.rsqrt(jnp.diagonal(gram_b) + 1e-06)
    normed_b = scales[:, None] * gram_b * scales[None, :]
    normed_a = scales[:, None] * sym_a * scales[None, :]
    lower = jnp.linalg.cholesky(normed_b)
    half_way = lower_solve(lower, normed_a)
    reduced = lower_solve(lower, half_way.T)
    shift = 2.0 * jnp.max(jnp.sum(jnp.abs(reduced), axis=1))
    iterate = jnp.eye(gram_a.shape[0], count, dtype=jnp.float32)
    for sweep_index in range(QSTEPS):
        iterate = shift * iterate - matmul(reduced, iterate)
        factor = jnp.linalg.cholesky(matmul(iterate.T, iterate))
        iterate = lower_solve(factor, iterate.T).T
    return scales[:, None] * upper_solve(lower, iterate)


def neighbour_sum(padded, coupled):
    rows_y = padded.shape[1] - 2
    rows_z = padded.shape[2] - 2
    rows_x = padded.shape[3] - 2
    total = jnp.zeros((padded.shape[0], rows_y, rows_z, rows_x), jnp.float32)
    for which, (step_y, step_z, step_x) in enumerate(offsets):
        ahead = padded[
            :,
            1 + step_y : 1 + step_y + rows_y,
            1 + step_z : 1 + step_z + rows_z,
            1 + step_x : 1 + step_x + rows_x,
        ]
        behind = padded[
            :,
            1 - step_y : 1 - step_y + rows_y,
            1 - step_z : 1 - step_z + rows_z,
            1 - step_x : 1 - step_x + rows_x,
        ]
        here = coupled[which, 1 : 1 + rows_y, 1 : 1 + rows_z, 1 : 1 + rows_x]
        back = coupled[
            which,
            1 - step_y : 1 - step_y + rows_y,
            1 - step_z : 1 - step_z + rows_z,
            1 - step_x : 1 - step_x + rows_x,
        ]
        total = total + here[None] * ahead
        total = total + back[None] * behind
    return total


def pad_plane(array):
    return jnp.pad(array, ((0, 0), (0, 0), (1, 1), (1, 1)))


def quotient(modes, images):
    total = lax.psum(matmul(modes, images.T), ("vox", "col"))
    return symmetric(total)


def on_device(start_modes, start_dirs, coupling, relax_class, relaxivity):
    local_voxels = coupling.shape[1]
    match = relax_class[:, None] == jnp.arange(relaxivity.shape[0], dtype=jnp.int32)[None, :]
    voxel_rate = jnp.sum(jnp.where(match, relaxivity[None, :], jnp.float32(0.0)), axis=1)
    damping = 1.0 / (1.0 + voxel_rate)
    own_coupling = coupling.reshape(HALF, 1, NZ, NX)
    before = from_behind(own_coupling, ("vox", "col"), 1)
    coupled = pad_plane(
        jnp.concatenate([before, own_coupling, jnp.zeros_like(own_coupling)], axis=1)
    )
    position = lax.axis_index(("vox", "col"))
    device_count = lax.axis_size(("vox", "col"))
    plane = jnp.ones((1, 1, NZ, NX), jnp.float32)
    upper_flag = (position > 0).astype(jnp.float32)
    lower_flag = (position < device_count - 1).astype(jnp.float32)
    unity = pad_plane(jnp.concatenate([upper_flag * plane, plane, lower_flag * plane], axis=1))
    degree = neighbour_sum(unity, coupled).reshape(local_voxels)
    diagonal = degree + voxel_rate

    def operate(field):
        count = field.shape[0]
        shaped = field.reshape(count, 1, NZ, NX)
        extended = extended_2(shaped, ((("vox", "col"), 1),), 1)
        padded = pad_plane(extended)
        return diagonal[None, :] * field - neighbour_sum(padded, coupled).reshape(
            count, local_voxels
        )

    modes, dirs = (
        lax.all_to_all(start_modes, "col", split_axis=1, concat_axis=0, tiled=True),
        lax.all_to_all(start_dirs, "col", split_axis=1, concat_axis=0, tiled=True),
    )
    count = modes.shape[0]
    images = operate(modes)
    dir_images = operate(dirs)
    ritz = quotient(modes, images)
    for iteration in range(ITERS):
        resid = images - matmul(ritz, modes)
        search = resid * damping[None, :]
        search_images = operate(search)
        basis = jnp.concatenate([modes, search, dirs], axis=0)
        basis_images = jnp.concatenate([images, search_images, dir_images], axis=0)
        local_a = matmul(basis, basis_images.T)
        local_b = matmul(basis, basis.T)
        gram_a, gram_b = lax.psum((local_a, local_b), ("vox", "col"))
        coeffs = project_pencil(gram_a, gram_b, count)
        modes = matmul(coeffs.T, basis)
        images = matmul(coeffs.T, basis_images)
        dirs = matmul(coeffs[count:].T, basis[count:])
        dir_images = matmul(coeffs[count:].T, basis_images[count:])
        ritz = quotient(modes, images)
    total_voxels = device_count * local_voxels
    scaled = modes * math.sqrt(total_voxels)
    modes_out = lax.all_to_all(scaled, "col", split_axis=0, concat_axis=1, tiled=True)
    return (modes_out, ritz)


def solution(mesh):
    in_specs = (P("col", "vox"), P("col", "vox"), P(None, ("vox", "col")), P(("vox", "col")), P())
    out_specs = (P("col", "vox"), P())
    return jax.shard_map(
        on_device, mesh=mesh, in_specs=in_specs, out_specs=out_specs, check_vma=False
    )
```

profile of v0, /device:TPU:1, one launch (start us, length us, event | category | flops | bytes accessed | tf_op | source)
XLA Modules:
  0.0 1733.3 jit_solution(11976527018198322847)
XLA Ops:
  8.8 6.6 all-to-all-start
  16.2 3.5 collective-permute-start
  25.2 4.1 all-to-all-start.1
  31.4 3.6 collective-permute-start.1
  36.0 2.9 collective-permute-start.6
  38.9 2.6 collective-permute-start.5
  41.6 2.3 select_maximum_fusion.6
  43.9 4.5 multiply_subtract_fusion.3
  49.6 3.4 select_maximum_fusion.2
  53.1 245.1 %all-reduce.15.cloned.1.call-done = f32[128,128]{0,1:T(8,128)} async-done(((f32[128,128]{0,1:T(8,128)}), f32[128,128]{0,1:T(8,128)}) %all-reduce.15.cloned.1.call-update) | async-done | bytes 65552 | tf_op jit(solution)/shard_map/psum | solution.py:104
  303.3 3.9 collective-permute-start.3
  307.2 5.4 fusion.64
  317.3 4.4 fusion.89
  325.0 256.1 %all-reduce.23.cloned.1.call-done = (f32[384,384]{1,0:T(8,128)}, f32[384,384]{0,1:T(8,128)}) async-done(((f32[384,384]{1,0:T(8,128)}, f32[384,384]{0,1:T(8,128)}), (f32[384,384]{1,0:T(8,128)}, f32[384,384]{0,1:T(8,128)})) %all-reduce.23.cloned.1.call-update) | async-done | bytes 1179664 | tf_op jit(solution)/shard_map/psum | solution.py:152
  581.2 6.6 gather_fusion
  590.4 11.7 cholesky.310
  602.2 9.8 custom-call.40
  614.4 11.7 cholesky.329
  626.2 9.9 custom-call.41
  637.5 11.7 cholesky.348
  652.6 5.9 while.12
  658.5 29.7 %custom-call.47 = f32[3,128,128]{1,2,0:T(8,128)S(1)} custom-call(f32[3,128,128]{2,1,0:T(8,128)S(1)} %get-tuple-element.49), custom_call_target="InvertDiagBlocksLowerTriangular" | custom-call | tf_op jit(solution)/shard_map/triangular_solve/custom-call.8 | solution.py:45
  695.7 11.7 cholesky.361
  708.7 9.8 custom-call.44
  720.8 11.7 cholesky.372
  733.9 9.8 custom-call.45
  745.5 11.9 cholesky.383
  758.7 9.8 custom-call.46
  773.6 237.5 %all-reduce.17.cloned.1.call-done = f32[128,128]{1,0:T(8,128)} async-done(((f32[128,128]{1,0:T(8,128)}), f32[128,128]{1,0:T(8,128)}) %all-reduce.17.cloned.1.call-update) | async-done | bytes 65552 | tf_op jit(solution)/shard_map/psum | solution.py:104
  1015.4 3.6 collective-permute-start.7
  1024.6 4.4 fusion.39
  1031.5 259.7 %all-reduce.21.cloned.1.call-done = (f32[384,384]{1,0:T(8,128)}, f32[384,384]{0,1:T(8,128)}) async-done(((f32[384,384]{1,0:T(8,128)}, f32[384,384]{0,1:T(8,128)}), (f32[384,384]{1,0:T(8,128)}, f32[384,384]{0,1:T(8,128)})) %all-reduce.21.cloned.1.call-update) | async-done | bytes 1179664 | tf_op jit(solution)/shard_map/psum | solution.py:152
  1291.2 6.6 gather_fusion.1
  1300.6 11.7 cholesky.396
  1312.4 9.8 custom-call.48
  1324.5 11.7 cholesky.415
  1336.3 10.2 custom-call.49
  1347.8 11.7 cholesky.434
  1363.5 6.4 while.13
  1369.9 29.7 %custom-call.55 = f32[3,128,128]{1,2,0:T(8,128)S(1)} custom-call(f32[3,128,128]{2,1,0:T(8,128)S(1)} %get-tuple-element.52), custom_call_target="InvertDiagBlocksLowerTriangular" | custom-call | tf_op jit(solution)/shard_map/triangular_solve/custom-call.8 | solution.py:45
  1407.1 11.7 cholesky.447
  1420.1 9.8 custom-call.52
  1432.0 11.7 cholesky.458
  1445.0 9.8 custom-call.53
  1456.7 11.9 cholesky.469
  1470.0 9.8 custom-call.54
  1485.0 7.1 all-to-all-start.2
  1492.1 231.0 %all-reduce.19.cloned.1.call-done = f32[128,128]{1,0:T(8,128)} async-done(((f32[128,128]{1,0:T(8,128)}), f32[128,128]{1,0:T(8,128)}) %all-reduce.19.cloned.1.call-update) | async-done | bytes 65552 | tf_op jit(solution)/shard_map/psum | solution.py:104
  (329 shorter events, 108.3 us)
Async XLA Ops:
  8.8 16.4 all-to-all-start
  16.2 8.8 collective-permute-start
  25.2 10.6 all-to-all-start.1
  29.3 268.9 %all-reduce.15.cloned.1.call-start = ((), (), s32[]{:S(2)}) async-start(), calls=%async_computation.3 | async-start | bytes 131072 | tf_op jit(solution)/shard_map/psum | solution.py:104
  29.5 12.1 collective-permute-start.2
  31.4 10.1 collective-permute-start.1
  35.1 13.3 copy-start.21
  35.1 13.3 copy-start.23
  35.1 13.3 copy-start.25
  35.1 13.3 copy-start.27
  35.2 13.3 copy-start.29
  35.2 13.3 copy-start.31
  35.2 13.3 copy-start.33
  35.8 17.2 copy-start.35
  36.0 12.5 copy-start.15
  36.0 13.6 collective-permute-start.6
  38.9 10.7 collective-permute-start.5
  49.6 531.6 %all-reduce.23.cloned.1.call-start = ((), (), s32[]{:S(2)}) async-start(), calls=%async_computation.7 | async-start | bytes 2359296 | tf_op jit(solution)/shard_map/psum | solution.py:152
  301.3 13.6 copy-start.16
  301.3 13.6 collective-permute-start.4
  303.3 11.6 collective-permute-start.3
  312.6 4.6 copy-start.22
  312.6 4.6 copy-start.24
  312.6 4.6 copy-start.26
  312.6 4.6 copy-start.28
  325.0 686.1 %all-reduce.17.cloned.1.call-start = ((), (), s32[]{:S(2)}) async-start(), calls=%async_computation.4 | async-start | bytes 131072 | tf_op jit(solution)/shard_map/psum | solution.py:104
  581.2 6.6 copy-start.2
  581.2 7.7 copy-start
  590.4 11.7 copy-start.12
  744.1 26.5 %copy-start.7 = (f32[128,512]{1,0:T(8,128)S(1)}, f32[128,512]{1,0:T(8,128)}, u32[]{:S(2)}) copy-start(f32[128,512]{1,0:T(8,128)} %copy-done.6) | copy-start | bytes 786436
  744.1 26.5 %copy-start.9 = (f32[128,512]{1,0:T(8,128)S(1)}, f32[128,512]{1,0:T(8,128)}, u32[]{:S(2)}) copy-start(f32[128,512]{1,0:T(8,128)} %copy-done.8) | copy-start | bytes 786436
  770.2 241.8 %copy-start.37 = (f32[512]{0:T(512)S(1)}, f32[512]{0:T(512)}, u32[]{:S(2)}) copy-start(f32[512]{0:T(512)} %get-tuple-element.163) | copy-start | bytes 6148
  771.3 257.8 %copy-start.4 = (f32[128,512]{1,0:T(8,128)}, f32[128,512]{1,0:T(8,128)S(1)}, u32[]{:S(2)}) copy-start(f32[128,512]{1,0:T(8,128)S(1)} %fusion.13) | copy-start | bytes 786436
  773.1 518.2 %all-reduce.21.cloned.1.call-start = ((), (), s32[]{:S(2)}) async-start(), calls=%async_computation.6 | async-start | bytes 2359296 | tf_op jit(solution)/shard_map/psum | solution.py:152
  773.6 255.6 %copy-start.10 = (f32[128,512]{1,0:T(8,128)}, f32[128,512]{1,0:T(8,128)S(1)}, u32[]{:S(2)}) copy-start(f32[128,512]{1,0:T(8,128)S(1)} %fusion.15) | copy-start | bytes 786436
  1013.5 8.3 collective-permute-start.8
  1015.4 6.9 collective-permute-start.7
  1019.5 9.7 copy-start.17
  1029.2 268.7 %copy-start.19 = (f32[128,512]{1,0:T(8,128)}, f32[128,512]{1,0:T(8,128)S(1)}, u32[]{:S(2)}) copy-start(f32[128,512]{1,0:T(8,128)S(1)} %multiply_subtract_fusion) | copy-start | bytes 786436
  1031.5 691.6 %all-reduce.19.cloned.1.call-start = ((), (), s32[]{:S(2)}) async-start(), calls=%async_computation.5 | async-start | bytes 131072 | tf_op jit(solution)/shard_map/psum | solution.py:104
  1291.2 6.7 copy-start.3
  1291.2 7.7 copy-start.1
  1300.5 11.7 copy-start.13
  1454.8 26.9 %copy-start.11 = (f32[128,512]{1,0:T(8,128)S(1)}, f32[128,512]{1,0:T(8,128)}, u32[]{:S(2)}) copy-start(f32[128,512]{1,0:T(8,128)} %copy-done.10) | copy-start | bytes 786436
  1455.9 27.2 %copy-start.5 = (f32[128,512]{1,0:T(8,128)S(1)}, f32[128,512]{1,0:T(8,128)}, u32[]{:S(2)}) copy-start(f32[128,512]{1,0:T(8,128)} %copy-done.4) | copy-start | bytes 786436
  1455.9 27.2 %copy-start.18 = (f32[128,512]{1,0:T(8,128)S(1)}, f32[128,512]{1,0:T(8,128)}, u32[]{:S(2)}) copy-start(f32[128,512]{1,0:T(8,128)} %copy-done.17) | copy-start | bytes 786436
  1455.9 27.2 %copy-start.20 = (f32[128,512]{1,0:T(8,128)S(1)}, f32[128,512]{1,0:T(8,128)}, u32[]{:S(2)}) copy-start(f32[128,512]{1,0:T(8,128)} %copy-done.19) | copy-start | bytes 786436
  1485.0 240.7 %all-to-all-start.2 = ((f32[8,16,512]{2,1,0:T(8,128)}), f32[8,16,512]{2,1,0:T(8,128)S(1)}, u32[]{:S(2)}, u32[]{:S(2)}) async-start(f32[8,16,512]{2,1,0:T(8,128)} %bitcast.87), calls=%async_computation.2 | async-start | bytes 524288 | tf_op jit(solution)/shard_map/all_to_all | solution.py:161
  (7 other events, 23.2 us)
Sparse Core Ops, SparseCore 0:
  49.7 248.4 all-reduce.14
  325.1 256.0 all-reduce.22
  773.2 237.8 all-reduce.16
  1031.6 259.5 all-reduce.20
  1485.1 237.9 all-reduce.18
where the time goes:
time: 1740 us; the launch traced here: 1730 us
  waiting for transfers between devices  1230 us (71%)
  other arithmetic  348 us (20%)
  matrix products  48.7 us (3%)
  starting transfers between devices  44.1 us (3%)
  local copies, waits for them, and re-layouts  41.4 us (2%)
  between operations  21 us (1%)
    psum x3, waiting for transfers between devices, quotient(): total = lax.psum(matmul(modes, images.T), ('vox', 'col'))  714 us
    psum x2, waiting for transfers between devices, on_device(): gram_a, gram_b = lax.psum((local_a, local_b), ('vox', 'col'))  516 us
    another operation x21, other arithmetic, project_pencil(): lower = jnp.linalg.cholesky(normed_b)  114 us
    another operation x18, other arithmetic, project_pencil(): factor = jnp.linalg.cholesky(matmul(iterate.T, iterate))  74.7 us
    another operation x12, other arithmetic, lower_solve(): return lax.linalg.triangular_solve(lower, rhs, left_side=True, lower=True)  62.8 us
    another operation x5, other arithmetic, upper_solve(): lax.linalg.triangular_solve(lower, rhs, left_side=True, lower=True, trans...  59.5 us
  transfers between devices with their start and end apart: 17, of which 6 were waited for; matrix products, arithmetic and copies ran while one was open for 2% of the time, Pallas kernels for 0%

commit v1 on v0

--- a/solution.py
+++ b/solution.py
@@ -149,7 +149,7 @@
         basis_images = jnp.concatenate([images, search_images, dir_images], axis=0)
         local_a = matmul(basis, basis_images.T)
         local_b = matmul(basis, basis.T)
-        gram_a, gram_b = lax.psum((local_a, local_b), ("vox", "col"))
+        gram_a, gram_b = lax.psum(lax.psum((local_a, local_b), axis_name="col"), axis_name="vox")
         coeffs = project_pencil(gram_a, gram_b, count)
         modes = matmul(coeffs.T, basis)
         images = matmul(coeffs.T, basis_images)

time: 1740 us -> 1660 us (0.954)
  waiting for transfers between devices: 1230 us -> 1150 us
    psum x2 -> x4, waiting for transfers between devices: 516 us -> 434 us  [the longest x2 300 us: on_device(): lax.psum(lax.psum((local_a, local_b), axis_name='col'), axis_name='vox')]
  transfers between devices with their start and end apart: 17 -> 19, of which waited for: 6 -> 8; matrix products, arithmetic and copies ran while one was open for 2% -> 2% of each run, Pallas kernels for 0% -> 0%
where the time goes in v1:
time: 1660 us
  waiting for transfers between devices  1150 us (69%)
  other arithmetic  348 us (21%)
  matrix products  48.7 us (3%)
  starting transfers between devices  46.6 us (3%)
  local copies, waits for them, and re-layouts  41.7 us (3%)
  between operations  21.3 us (1%)
    psum x3, waiting for transfers between devices, quotient(): total = lax.psum(matmul(modes, images.T), ('vox', 'col'))  715 us
    psum x2, waiting for transfers between devices, on_device(): lax.psum(lax.psum((local_a, local_b), axis_name='col'), axis_name='vox')  300 us
    psum x2, waiting for transfers between devices, on_device(): lax.psum((local_a, local_b), axis_name='col')  135 us
    another operation x21, other arithmetic, project_pencil(): lower = jnp.linalg.cholesky(normed_b)  114 us
    another operation x18, other arithmetic, project_pencil(): factor = jnp.linalg.cholesky(matmul(iterate.T, iterate))  74.7 us
    another operation x12, other arithmetic, lower_solve(): return lax.linalg.triangular_solve(lower, rhs, left_side=True, lower=True)  62.8 us
    another operation x5, other arithmetic, upper_solve(): lax.linalg.triangular_solve(lower, rhs, left_side=True, lower=True, trans...  59.5 us
  transfers between devices with their start and end apart: 19, of which 8 were waited for; matrix products, arithmetic and copies ran while one was open for 2% of the time, Pallas kernels for 0%

profile of v1, /device:TPU:1, one launch (start us, length us, event | category | flops | bytes accessed | tf_op | source)
XLA Modules:
  0.0 1656.5 jit_solution(1726911456861507876)
XLA Ops:
  8.8 6.6 all-to-all-start
  16.2 3.5 collective-permute-start
  25.2 4.1 all-to-all-start.1
  31.4 3.6 collective-permute-start.1
  36.0 2.9 collective-permute-start.6
  43.9 4.5 multiply_subtract_fusion.3
  49.6 3.4 select_maximum_fusion.2
  53.1 245.1 %all-reduce.19.cloned.1.call-done = f32[128,128]{0,1:T(8,128)} async-done(((f32[128,128]{0,1:T(8,128)}), f32[128,128]{0,1:T(8,128)}) %all-reduce.19.cloned.1.call-update) | async-done | bytes 65552 | tf_op jit(solution)/shard_map/psum | solution.py:104
  303.3 3.9 collective-permute-start.3
  307.1 5.4 fusion.64
  317.3 4.4 fusion.89
  325.0 65.6 %all-reduce.31.cloned.1.call-done = (f32[384,384]{1,0:T(8,128)}, f32[384,384]{0,1:T(8,128)}) async-done(((f32[384,384]{1,0:T(8,128)}, f32[384,384]{0,1:T(8,128)}), (f32[384,384]{1,0:T(8,128)}, f32[384,384]{0,1:T(8,128)})) %all-reduce.31.cloned.1.call-update) | async-done | bytes 1179664 | tf_op jit(solution)/shard_map/psum | solution.py:152
  390.7 150.0 %all-reduce.27.cloned.1.call-done = (f32[384,384]{1,0:T(8,128)}, f32[384,384]{0,1:T(8,128)}) async-done(((f32[384,384]{1,0:T(8,128)}, f32[384,384]{0,1:T(8,128)}), (f32[384,384]{1,0:T(8,128)}, f32[384,384]{0,1:T(8,128)})) %all-reduce.27.cloned.1.call-update) | async-done | bytes 1179664 | tf_op jit(solution)/shard_map/psum | solution.py:152
  540.7 6.8 gather_fusion
  550.2 11.7 cholesky.310
  562.0 9.8 custom-call.40
  574.2 11.7 cholesky.329
  585.9 9.9 custom-call.41
  597.2 11.7 cholesky.348
  612.3 5.9 while.12
  618.2 29.7 %custom-call.47 = f32[3,128,128]{1,2,0:T(8,128)S(1)} custom-call(f32[3,128,128]{2,1,0:T(8,128)S(1)} %get-tuple-element.49), custom_call_target="InvertDiagBlocksLowerTriangular" | custom-call | tf_op jit(solution)/shard_map/triangular_solve/custom-call.8 | solution.py:45
  655.4 11.7 cholesky.361
  668.5 9.8 custom-call.44
  680.6 11.7 cholesky.372
  693.6 9.8 custom-call.45
  705.3 11.9 cholesky.383
  718.5 9.8 custom-call.46
  733.3 239.5 %all-reduce.21.cloned.1.call-done = f32[128,128]{1,0:T(8,128)} async-done(((f32[128,128]{1,0:T(8,128)}), f32[128,128]{1,0:T(8,128)}) %all-reduce.21.cloned.1.call-update) | async-done | bytes 65552 | tf_op jit(solution)/shard_map/psum | solution.py:104
  977.2 3.6 collective-permute-start.7
  986.4 4.4 fusion.39
  993.3 69.0 %all-reduce.29.cloned.1.call-done = (f32[384,384]{1,0:T(8,128)}, f32[384,384]{0,1:T(8,128)}) async-done(((f32[384,384]{1,0:T(8,128)}, f32[384,384]{0,1:T(8,128)}), (f32[384,384]{1,0:T(8,128)}, f32[384,384]{0,1:T(8,128)})) %all-reduce.29.cloned.1.call-update) | async-done | bytes 1179664 | tf_op jit(solution)/shard_map/psum | solution.py:152
  1062.4 149.9 %all-reduce.25.cloned.1.call-done = (f32[384,384]{1,0:T(8,128)}, f32[384,384]{0,1:T(8,128)}) async-done(((f32[384,384]{1,0:T(8,128)}, f32[384,384]{0,1:T(8,128)}), (f32[384,384]{1,0:T(8,128)}, f32[384,384]{0,1:T(8,128)})) %all-reduce.25.cloned.1.call-update) | async-done | bytes 1179664 | tf_op jit(solution)/shard_map/psum | solution.py:152
  1212.2 6.7 gather_fusion.1
  1221.6 11.7 cholesky.396
  1233.4 9.8 custom-call.48
  1245.6 11.7 cholesky.415
  1257.3 10.2 custom-call.49
  1268.8 11.7 cholesky.434
  1284.5 6.4 while.13
  1290.9 29.7 %custom-call.55 = f32[3,128,128]{1,2,0:T(8,128)S(1)} custom-call(f32[3,128,128]{2,1,0:T(8,128)S(1)} %get-tuple-element.52), custom_call_target="InvertDiagBlocksLowerTriangular" | custom-call | tf_op jit(solution)/shard_map/triangular_solve/custom-call.8 | solution.py:45
  1328.1 11.7 cholesky.447
  1341.1 9.8 custom-call.52
  1353.0 11.7 cholesky.458
  1366.0 9.8 custom-call.53
  1377.7 11.9 cholesky.469
  1391.0 9.8 custom-call.54
  1406.0 9.6 all-to-all-start.2
  1415.6 230.5 %all-reduce.23.cloned.1.call-done = f32[128,128]{1,0:T(8,128)} async-done(((f32[128,128]{1,0:T(8,128)}), f32[128,128]{1,0:T(8,128)}) %all-reduce.23.cloned.1.call-update) | async-done | bytes 65552 | tf_op jit(solution)/shard_map/psum | solution.py:104
  (335 shorter events, 113.3 us)
Async XLA Ops:
  8.8 16.4 all-to-all-start
  16.2 8.8 collective-permute-start
  25.2 10.6 all-to-all-start.1
  29.3 268.9 %all-reduce.19.cloned.1.call-start = ((), (), s32[]{:S(2)}) async-start(), calls=%async_computation.3 | async-start | bytes 131072 | tf_op jit(solution)/shard_map/psum | solution.py:104
  29.5 12.1 collective-permute-start.2
  31.4 10.1 collective-permute-start.1
  35.1 13.3 copy-start.21
  35.1 13.3 copy-start.23
  35.1 13.3 copy-start.25
  35.1 13.3 copy-start.27
  35.2 13.3 copy-start.29
  35.2 13.3 copy-start.31
  35.2 13.3 copy-start.33
  35.8 17.2 %copy-start.35 = (f32[512]{0:T(512)}, f32[512]{0:T(512)S(1)}, u32[]{:S(2)}) copy-start(f32[512]{0:T(512)S(1)} %get-tuple-element.168) | copy-start | bytes 6148
  36.0 12.5 copy-start.15
  36.0 13.6 collective-permute-start.6
  38.9 10.7 collective-permute-start.5
  49.5 341.0 %all-reduce.31.cloned.1.call-start = ((), (), s32[]{:S(2)}) async-start(), calls=%async_computation.9 | async-start | bytes 2359296 | tf_op jit(solution)/shard_map/psum | solution.py:152
  301.2 13.6 copy-start.16
  301.2 13.6 collective-permute-start.4
  303.3 11.6 collective-permute-start.3
  312.6 4.6 copy-start.22
  312.6 4.6 copy-start.24
  324.9 215.8 %all-reduce.27.cloned.1.call-start = ((), (), s32[]{:S(2)}) async-start(), calls=%async_computation.7 | async-start | bytes 2359296 | tf_op jit(solution)/shard_map/psum | solution.py:152
  390.6 582.3 %all-reduce.21.cloned.1.call-start = ((), (), s32[]{:S(2)}) async-start(), calls=%async_computation.4 | async-start | bytes 131072 | tf_op jit(solution)/shard_map/psum | solution.py:104
  540.7 6.8 copy-start.2
  540.7 7.9 copy-start
  550.1 11.7 copy-start.12
  703.8 26.5 %copy-start.7 = (f32[128,512]{1,0:T(8,128)S(1)}, f32[128,512]{1,0:T(8,128)}, u32[]{:S(2)}) copy-start(f32[128,512]{1,0:T(8,128)} %copy-done.6) | copy-start | bytes 786436
  703.9 26.5 %copy-start.9 = (f32[128,512]{1,0:T(8,128)S(1)}, f32[128,512]{1,0:T(8,128)}, u32[]{:S(2)}) copy-start(f32[128,512]{1,0:T(8,128)} %copy-done.8) | copy-start | bytes 786436
  729.9 243.8 %copy-start.37 = (f32[512]{0:T(512)S(1)}, f32[512]{0:T(512)}, u32[]{:S(2)}) copy-start(f32[512]{0:T(512)} %get-tuple-element.167) | copy-start | bytes 6148
  731.0 259.9 %copy-start.4 = (f32[128,512]{1,0:T(8,128)}, f32[128,512]{1,0:T(8,128)S(1)}, u32[]{:S(2)}) copy-start(f32[128,512]{1,0:T(8,128)S(1)} %fusion.13) | copy-start | bytes 786436
  732.8 329.5 %all-reduce.29.cloned.1.call-start = ((), (), s32[]{:S(2)}) async-start(), calls=%async_computation.8 | async-start | bytes 2359296 | tf_op jit(solution)/shard_map/psum | solution.py:152
  733.3 257.6 %copy-start.10 = (f32[128,512]{1,0:T(8,128)}, f32[128,512]{1,0:T(8,128)S(1)}, u32[]{:S(2)}) copy-start(f32[128,512]{1,0:T(8,128)S(1)} %fusion.15) | copy-start | bytes 786436
  975.2 8.3 collective-permute-start.8
  977.2 6.9 collective-permute-start.7
  981.3 9.6 copy-start.17
  990.9 228.0 %copy-start.19 = (f32[128,512]{1,0:T(8,128)}, f32[128,512]{1,0:T(8,128)S(1)}, u32[]{:S(2)}) copy-start(f32[128,512]{1,0:T(8,128)S(1)} %multiply_subtract_fusion) | copy-start | bytes 786436
  993.2 219.0 %all-reduce.25.cloned.1.call-start = ((), (), s32[]{:S(2)}) async-start(), calls=%async_computation.6 | async-start | bytes 2359296 | tf_op jit(solution)/shard_map/psum | solution.py:152
  1062.3 583.7 %all-reduce.23.cloned.1.call-start = ((), (), s32[]{:S(2)}) async-start(), calls=%async_computation.5 | async-start | bytes 131072 | tf_op jit(solution)/shard_map/psum | solution.py:104
  1212.2 6.7 copy-start.3
  1212.2 7.8 copy-start.1
  1221.6 11.7 copy-start.13
  1375.9 26.9 %copy-start.11 = (f32[128,512]{1,0:T(8,128)S(1)}, f32[128,512]{1,0:T(8,128)}, u32[]{:S(2)}) copy-start(f32[128,512]{1,0:T(8,128)} %copy-done.10) | copy-start | bytes 786436
  1376.9 27.3 %copy-start.5 = (f32[128,512]{1,0:T(8,128)S(1)}, f32[128,512]{1,0:T(8,128)}, u32[]{:S(2)}) copy-start(f32[128,512]{1,0:T(8,128)} %copy-done.4) | copy-start | bytes 786436
  1376.9 27.2 %copy-start.18 = (f32[128,512]{1,0:T(8,128)S(1)}, f32[128,512]{1,0:T(8,128)}, u32[]{:S(2)}) copy-start(f32[128,512]{1,0:T(8,128)} %copy-done.17) | copy-start | bytes 786436
  1377.0 27.2 %copy-start.20 = (f32[128,512]{1,0:T(8,128)S(1)}, f32[128,512]{1,0:T(8,128)}, u32[]{:S(2)}) copy-start(f32[128,512]{1,0:T(8,128)} %copy-done.19) | copy-start | bytes 786436
  1406.0 242.6 %all-to-all-start.2 = ((f32[8,16,512]{2,1,0:T(8,128)}), f32[8,16,512]{2,1,0:T(8,128)S(1)}, u32[]{:S(2)}, u32[]{:S(2)}) async-start(f32[8,16,512]{2,1,0:T(8,128)} %bitcast.87), calls=%async_computation.2 | async-start | bytes 524288 | tf_op jit(solution)/shard_map/all_to_all | solution.py:161
  (9 other events, 32.4 us)
Sparse Core Ops, SparseCore 0:
  49.7 248.4 all-reduce.18
  325.0 65.4 all-reduce.30
  394.0 146.5 all-reduce.26
  732.9 239.8 all-reduce.20
  993.4 68.8 all-reduce.28
  1065.6 146.5 all-reduce.24
  1406.1 239.8 all-reduce.22
